TPU v7x, 32 devices: a whole 2x2x4 slice. The times are simulated.
32 devices in a mesh: batch: 16 (over z, x, core), head: 2 (over y).
Axes of the slice: x: 2, y: 2, z: 4, core: 2. Of those that a mesh axis runs over, the one named last changes fastest.
Arguments:
- inputs: bfloat16 [32, 16, 44, 256], P(('batch', 'head')), may hold values from -12 to 12
- cot_shared: bfloat16 [32, 8, 22, 512], P(('batch', 'head')), may hold values from -5 to 5
- cot_task: bfloat16 [2, 32, 8, 22, 512], P('head', 'batch'), may hold values from -6 to 6
- trunk_one: float32 [1179648], P(('batch', 'head')), may hold values from -0.125 to 0.125
- trunk_one_first: float32 [1179648], P(('batch', 'head')), may hold values from -20 to 20
- trunk_one_second: float32 [1179648], P(('batch', 'head')), may hold values from 0.90112 to 3.60448
- attention: float32 [2, 524288], P('head', 'batch'), may hold values from -0.25 to 0.25
- attention_first: float32 [2, 524288], P('head', 'batch'), may hold values from -4 to 4
- attention_second: float32 [2, 524288], P('head', 'batch'), may hold values from 0.00518144 to 0.0202752
- head_conv: float32 [2, 2359296], P('head', 'batch'), may hold values from -0.09375 to 0.09375
- head_conv_first: float32 [2, 2359296], P('head', 'batch'), may hold values from -4 to 4
- head_conv_second: float32 [2, 2359296], P('head', 'batch'), may hold values from 0.0946176 to 0.382976
- norm_params: float32 [2, 512], replicated, may hold values from -0.6 to 1.5
- norm_first: float32 [2, 512], replicated, may hold values from -2048 to 2048
- norm_second: float32 [2, 512], replicated, may hold values from 5075.108 to 81201.73
Outputs:
- shared_out: float32 [32, 8, 22, 512], P(('batch', 'head'))
- task_out: float32 [2, 32, 8, 22, 512], P('head', 'batch')
- input_grad: float32 [32, 16, 44, 256], P(('batch', 'head'))
- trunk_one_next: float32 [1179648], P(('batch', 'head'))
- trunk_one_first_next: float32 [1179648], P(('batch', 'head'))
- trunk_one_second_next: float32 [1179648], P(('batch', 'head'))
- attention_next: float32 [2, 524288], P('head', 'batch')
- attention_first_next: float32 [2, 524288], P('head', 'batch')
- attention_second_next: float32 [2, 524288], P('head', 'batch')
- head_conv_next: float32 [2, 2359296], P('head', 'batch')
- head_conv_first_next: float32 [2, 2359296], P('head', 'batch')
- head_conv_second_next: float32 [2, 2359296], P('head', 'batch')
- norm_next: float32 [2, 512], replicated
- norm_first_next: float32 [2, 512], replicated
- norm_second_next: float32 [2, 512], replicated
All inputs are finite; a program needn't handle non-finite values.
Results may differ from a plain program's by a relative error of at most 0.0068.
Values may be sent and summed in bfloat16 or wider, within the bound.
No kernel may reach another device: no remote copies, remote signals or barrier semaphores. Data moves between devices by JAX's collectives and lax.ppermute only.
A program may use at most 128 MiB of HBM per device.

v0:
```python
import jax
import jax.numpy as jnp
from jax import lax
from jax.sharding import PartitionSpec as P

STEP = 10


EPS_NORM = 1e-05
BETA_FIRST = 0.9
BETA_SECOND = 0.999
ADAM_EPS = 1e-08
RATE_MATRIX = 0.02
RATE_NORM = 0.4
WEIGHT_DECAY = 0.01


def pad_field(field):
    return jnp.pad(field, ((0, 0), (1, 1), (1, 1), (0, 0)))


def conv_apply(field_low, kernel_low):
    padded = pad_field(field_low)
    height = field_low.shape[1]
    breadth = field_low.shape[2]
    summed = jnp.zeros(field_low.shape[:3] + (kernel_low.shape[2],), jnp.float32)
    for tap_index in range(9):
        tap_down = tap_index // 3
        tap_across = tap_index % 3
        window = padded[:, tap_down : tap_down + height, tap_across : tap_across + breadth, :]
        summed = summed + jnp.einsum(
            "fhwc,cd->fhwd", window, kernel_low[tap_index], preferred_element_type=jnp.float32
        )
    return summed


def conv_input_grad(grad_low, kernel_low):
    padded = pad_field(grad_low)
    height = grad_low.shape[1]
    breadth = grad_low.shape[2]
    summed = jnp.zeros(grad_low.shape[:3] + (kernel_low.shape[1],), jnp.float32)
    for tap_index in range(9):
        tap_down = tap_index // 3
        tap_across = tap_index % 3
        window = padded[
            :, 2 - tap_down : 2 - tap_down + height, 2 - tap_across : 2 - tap_across + breadth, :
        ]
        summed = summed + jnp.einsum(
            "fhwd,cd->fhwc", window, kernel_low[tap_index], preferred_element_type=jnp.float32
        )
    return summed


def conv_kernel_grad(field_low, grad_low):
    padded = pad_field(field_low)
    height = field_low.shape[1]
    breadth = field_low.shape[2]
    tap_grads = []
    for tap_index in range(9):
        tap_down = tap_index // 3
        tap_across = tap_index % 3
        window = padded[:, tap_down : tap_down + height, tap_across : tap_across + breadth, :]
        tap_grads.append(
            jnp.einsum("fhwc,fhwd->cd", window, grad_low, preferred_element_type=jnp.float32)
        )
    return jnp.stack(tap_grads)


def mean_pool(values):
    frames, height, breadth, channels = values.shape
    return jnp.mean(values.reshape(frames, height // 2, 2, breadth // 2, 2, channels), axis=(2, 4))


def pool_back(gradient):
    frames, half_down, half_across, channels = gradient.shape
    spread = jnp.broadcast_to(
        gradient[:, :, None, :, None, :] * 0.25, (frames, half_down, 2, half_across, 2, channels)
    )
    return spread.reshape(frames, half_down * 2, half_across * 2, channels)


def gelu_back(at_point, gradient):
    return jax.vjp(jax.nn.gelu, at_point)[1](gradient)[0]


def adamw(weight, first_state, second_state, gradient, step_rate):
    first_next = BETA_FIRST * first_state + (1.0 - BETA_FIRST) * gradient
    second_next = BETA_SECOND * second_state + (1.0 - BETA_SECOND) * gradient * gradient
    first_fix = 1.0 - BETA_FIRST**STEP
    second_fix = 1.0 - BETA_SECOND**STEP
    update = first_next / first_fix / (jnp.sqrt(second_next / second_fix) + ADAM_EPS)
    return (weight - step_rate * (update + WEIGHT_DECAY * weight), first_next, second_next)


def body(
    inputs,
    cot_shared,
    cot_task,
    trunk_one,
    trunk_one_first,
    trunk_one_second,
    attention,
    attention_first,
    attention_second,
    head_conv,
    head_conv_first,
    head_conv_second,
    norm_params,
    norm_first,
    norm_second,
):
    channels_in = inputs.shape[3]
    channels = norm_params.shape[1]
    total_count = float(
        inputs.shape[0]
        * inputs.shape[1]
        * inputs.shape[2]
        * lax.axis_size("batch")
        * lax.axis_size("head")
    )
    one_low = lax.all_gather(trunk_one.astype(jnp.bfloat16), ("batch", "head"), axis=0, tiled=True)
    kernel_one = one_low.reshape(9, channels_in, channels)
    attention_low, head_low = (
        lax.all_gather(attention.astype(jnp.bfloat16), "batch", axis=1, tiled=True),
        lax.all_gather(head_conv.astype(jnp.bfloat16), "batch", axis=1, tiled=True),
    )
    attention_mat = attention_low.reshape(2, channels, channels)
    head_mat = head_low.reshape(9, channels, channels)
    field_one = conv_apply(inputs, kernel_one)
    local_sum = jnp.sum(field_one, axis=(0, 1, 2))
    local_square = jnp.sum(field_one * field_one, axis=(0, 1, 2))
    total_sum, total_square = lax.psum((local_sum, local_square), ("batch", "head"))
    center = total_sum / total_count
    spread = total_square / total_count - center * center
    inverse = lax.rsqrt(spread + EPS_NORM)
    normed = (field_one - center) * inverse
    pre_act = norm_params[0] * normed + norm_params[1]
    section = jax.nn.gelu(pre_act).astype(jnp.bfloat16)
    shared_out = mean_pool(section.astype(jnp.float32))
    gathered = lax.all_gather(section, "head", axis=0, tiled=True)
    inner_field = jnp.einsum(
        "fhwc,cd->fhwd", gathered, attention_mat[0], preferred_element_type=jnp.float32
    )
    activated = jax.nn.gelu(inner_field).astype(jnp.bfloat16)
    logits = jnp.einsum(
        "fhwc,cd->fhwd", activated, attention_mat[1], preferred_element_type=jnp.float32
    )
    mask_field = jax.nn.sigmoid(logits)
    wide_section = gathered.astype(jnp.float32)
    masked = (mask_field * wide_section).astype(jnp.bfloat16)
    head_field = conv_apply(masked, head_mat)
    task_out = mean_pool(jax.nn.gelu(head_field))
    grad_head = gelu_back(head_field, pool_back(cot_task[0].astype(jnp.float32))).astype(
        jnp.bfloat16
    )
    grad_head_kernel = conv_kernel_grad(masked, grad_head)
    grad_masked = conv_input_grad(grad_head, head_mat)
    grad_logits = (grad_masked * wide_section * mask_field * (1.0 - mask_field)).astype(
        jnp.bfloat16
    )
    grad_second_att = jnp.einsum(
        "fhwc,fhwd->cd", activated, grad_logits, preferred_element_type=jnp.float32
    )
    grad_activated = jnp.einsum(
        "fhwd,cd->fhwc", grad_logits, attention_mat[1], preferred_element_type=jnp.float32
    )
    grad_inner = gelu_back(inner_field, grad_activated).astype(jnp.bfloat16)
    grad_first_att = jnp.einsum(
        "fhwc,fhwd->cd", gathered, grad_inner, preferred_element_type=jnp.float32
    )
    feature_back = (
        jnp.einsum(
            "fhwd,cd->fhwc", grad_inner, attention_mat[0], preferred_element_type=jnp.float32
        )
        + grad_masked * mask_field
    )
    back_section = lax.psum_scatter(feature_back, "head", scatter_dimension=0, tiled=True)
    att_grad = jnp.stack([grad_first_att, grad_second_att]).reshape(1, -1)
    att_share, head_share = (
        lax.psum_scatter(att_grad, "batch", scatter_dimension=1, tiled=True),
        lax.psum_scatter(grad_head_kernel.reshape(1, -1), "batch", scatter_dimension=1, tiled=True),
    )
    grad_section = pool_back(cot_shared.astype(jnp.float32)) + back_section
    grad_pre = gelu_back(pre_act, grad_section)
    local_plain = jnp.sum(grad_pre, axis=(0, 1, 2))
    local_cross = jnp.sum(grad_pre * normed, axis=(0, 1, 2))
    plain_sum, cross_sum = lax.psum((local_plain, local_cross), ("batch", "head"))
    grad_field = (
        norm_params[0]
        * inverse
        * (grad_pre - plain_sum / total_count - normed * cross_sum / total_count)
    ).astype(jnp.bfloat16)
    grad_kernel_one = conv_kernel_grad(inputs, grad_field)
    input_grad = conv_input_grad(grad_field, kernel_one)
    one_share = lax.psum_scatter(
        grad_kernel_one.reshape(-1), ("batch", "head"), scatter_dimension=0, tiled=True
    )
    norm_grad = jnp.stack([cross_sum, plain_sum])
    one_new = adamw(trunk_one, trunk_one_first, trunk_one_second, one_share, RATE_MATRIX)
    att_new = adamw(attention, attention_first, attention_second, att_share, RATE_MATRIX)
    head_new = adamw(head_conv, head_conv_first, head_conv_second, head_share, RATE_MATRIX)
    norm_new = adamw(norm_params, norm_first, norm_second, norm_grad, RATE_NORM)
    return (
        shared_out,
        task_out[None],
        input_grad,
        one_new[0],
        one_new[1],
        one_new[2],
        att_new[0],
        att_new[1],
        att_new[2],
        head_new[0],
        head_new[1],
        head_new[2],
        norm_new[0],
        norm_new[1],
        norm_new[2],
    )


def solution(mesh):
    in_specs = (
        P(("batch", "head"), None, None, None),
        P(("batch", "head"), None, None, None),
        P("head", "batch", None, None, None),
        P(("batch", "head")),
        P(("batch", "head")),
        P(("batch", "head")),
        P("head", "batch"),
        P("head", "batch"),
        P("head", "batch"),
        P("head", "batch"),
        P("head", "batch"),
        P("head", "batch"),
        P(),
        P(),
        P(),
    )
    out_specs = (
        P(("batch", "head"), None, None, None),
        P("head", "batch", None, None, None),
        P(("batch", "head"), None, None, None),
        P(("batch", "head")),
        P(("batch", "head")),
        P(("batch", "head")),
        P("head", "batch"),
        P("head", "batch"),
        P("head", "batch"),
        P("head", "batch"),
        P("head", "batch"),
        P("head", "batch"),
        P(),
        P(),
        P(),
    )
    return jax.shard_map(body, mesh=mesh, in_specs=in_specs, out_specs=out_specs, check_vma=False)
```

profile of v0, /device:TPU:0, one launch (start us, length us, event | category | flops | bytes accessed | tf_op | source)
XLA Modules:
  0.0 780.7 jit_solution(17294030770670349669)
XLA Ops:
  12.4 59.1 %all-gather.6.cloned.1.call-done = bf16[1179648]{0:T(1024)(128)(2,1)} async-done(((bf16[36864]{0:T(1024)(128)(2,1)}), bf16[1179648]{0:T(1024)(128)(2,1)}) %all-gather.6.cloned.1.call-update) | async-done | bytes 2359312 | tf_op jit(solution)/shard_map/all_gather | solution.py:121
  71.6 2.6 fusion.338
  90.9 39.0 %all-reduce.8 = (f32[512]{0:T(512)S(1)}, f32[512]{0:T(512)S(1)}) all-reduce(f32[512]{0:T(512)S(1)} %get-tuple-element.74, f32[512]{0:T(512)S(1)} %get-tuple-element.73), channel_id=1, replica_groups=mesh['batch'=16,'head'=2] {'batch','head'}, use_global_device_ids=true, to_apply=%region_3.4 | all-reduce | flops 1024 | bytes 8192 | tf_op jit(solution)/shard_map/psum | solution.py:132
  136.4 12.3 %slice_reduce_fusion.10 = (bf16[262144]{0:T(1024)(128)(2,1)S(1)}, bf16[262144]{0:T(1024)(128)(2,1)S(1)}) fusion(bf16[1,524288]{1,0:T(2,128)(2,1)} %all-gather.8.cloned.1.call-done), kind=kLoop, calls=%fused_computation.159 | loop fusion | bytes 2097152 | tf_op jit(solution)/shard_map/slice | solution.py:142
  149.4 10.1 %all-gather.12.cloned.1.call-done = bf16[32,44,512]{2,0,1:T(8,128)(2,1)} async-done(((bf16[16,44,512]{2,0,1:T(8,128)(2,1)}), bf16[32,44,512]{2,0,1:T(8,128)(2,1)}) %all-gather.12.cloned.1.call-update) | async-done | bytes 1441808 | tf_op jit(solution)/shard_map/all_gather | solution.py:140
  159.5 2.2 copy.52
  164.6 3.0 fusion
  167.6 76.0 %all-gather.10.cloned.1.call-done = bf16[1,2359296]{1,0:T(2,128)(2,1)} async-done(((bf16[1,147456]{1,0:T(2,128)(2,1)}), bf16[1,2359296]{1,0:T(2,128)(2,1)}) %all-gather.10.cloned.1.call-update) | async-done | bytes 4718608 | tf_op jit(solution)/shard_map/all_gather | solution.py:125
  243.7 37.3 %slice_reduce_fusion = (bf16[262144]{0:T(1024)(128)(2,1)S(1)}, bf16[262144]{0:T(1024)(128)(2,1)S(1)}, bf16[262144]{0:T(1024)(128)(2,1)}, bf16[262144]{0:T(1024)(...) fusion(bf16[1,2359296]{1,0:T(2,128)(2,1)} %all-gather.10.cloned, ...), kind=kLoop, calls=%fused_computation.149 | loop fusion | bytes 9437184 | tf_op jit(solution)/shard_map/slice | solution.py:32
  283.9 2.6 fusion.50
  286.6 2.6 fusion.54
  290.6 2.7 fusion.58
  293.6 2.7 fusion.181
  296.6 2.7 fusion.62
  299.6 2.7 fusion.66
  302.7 2.6 fusion.74
  309.3 9.2 %fusion.17 = (bf16[2,16,44,512]{3,2,1,0:T(8,128)(2,1)S(1)}, f32[2,16,44,512]{3,2,1,0:T(8,128)}) fusion(f32[2,16,44,512]{3,0,2,1:T(2,128)S(1)} %bitcast.386, bf16[512,512,1,1]{1,0,2,3:T(8,128)(2,1)S(1)} %copy-done.14, bf16[2,16,44,512]{3,2,1,0:T(8,128)(2,1)S(1)} %get-tuple-element.111, f32[2,16,44,512]{3,2,1,0:T(8,128)S(1)} %copy-done.5, ...), kind=kOutput, calls=%fused_computation.23 | convolution fusion | flops 759103488 | bytes 32243712 | tf_op jit(solution)/shard_map/fhwc,cd->fhwd/dot_general | solution.py:31
  322.7 2.6 fusion.37
  325.4 2.7 fusion.39
  328.1 2.7 fusion.43
  330.8 2.7 fusion.41
  333.5 8.7 %fusion.3 = (bf16[2,16,44,512]{3,2,1,0:T(8,128)(2,1)}, f32[2,16,44,512]{3,2,1,0:T(8,128)}) fusion(f32[2,16,44,512]{3,2,1,0:T(8,128)} %get-tuple-element.112, bf16[2,16,44,512]{3,2,1,0:T(8,128)(2,1)S(1)} %bitcast.383, bf16[512,512,1,1]{1,0,2,3:T(8,128)(2,1)} %reshape.409, bf16[2,16,44,512]{3,2,1,0:T(8,128)(2,1)S(1)} %get-tuple-element.94, ...), kind=kOutput, calls=%fused_computation.9 | convolution fusion | flops 748290048 | bytes 33685504 | tf_op jit(solution)/shard_map/fhwd,cd->fhwc/dot_general | solution.py:48
  342.2 5.4 fusion.10
  347.6 2.1 convolution_bitcast_fusion.2
  349.7 2.8 multiply_add_fusion
  353.0 3.8 convolution_bitcast_fusion.1
  358.3 5.5 reshape.385
  363.8 2.0 fusion.79
  367.7 2.1 fusion.91
  369.8 2.0 fusion.97
  371.8 2.0 fusion.124
  373.8 2.0 fusion.103
  375.8 2.0 fusion.109
  377.8 2.0 fusion.115
  379.8 2.0 fusion.121
  381.8 20.6 %reshape.386 = f32[1,2359296]{1,0:T(1,128)} reshape(f32[9,512,512]{2,1,0:T(8,128)} %fusion.121) | data formatting | bytes 18874368 | tf_op jit(solution)/shard_map/reshape | solution.py:181
  404.0 2.1 broadcast_in_dim.7
  408.0 3.1 reshape.439
  411.1 3.1 reduce_sum.56
  416.2 3.9 copy.53
  420.1 3.5 reduce_sum.57
  425.0 4.8 fusion.331
  429.8 41.3 %all-reduce.7 = (f32[512]{0:T(512)S(1)}, f32[512]{0:T(512)S(1)}) all-reduce(f32[512]{0:T(512)S(1)} %get-tuple-element.72, f32[512]{0:T(512)S(1)} %get-tuple-element.71), channel_id=1, replica_groups=mesh['batch'=16,'head'=2] {'batch','head'}, use_global_device_ids=true, to_apply=%region_10.11 | all-reduce | flops 1024 | bytes 8192 | tf_op jit(solution)/shard_map/psum | solution.py:187
  477.2 3.4 copy.92
  480.7 139.7 %all-reduce.15.cloned.1.call-done = (f32[1,524288]{1,0:T(1,128)}, f32[1,2359296]{1,0:T(1,128)}) async-done(((f32[1,524288]{1,0:T(1,128)}, f32[1,2359296]{1,0:T(1,128)}), (f32[1,524288]{1,0:T(1,128)}, f32[1,2359296]{1,0:T(1,128)})) %all-reduce.15.cloned.1.call-update) | async-done | bytes 11534352
  620.4 2.5 multiply_subtract_fusion.2
  623.0 6.1 multiply_subtract_fusion
  639.1 132.6 %all-reduce.13.cloned.1.call-done = f32[1179648]{0:T(1024)} async-done(((f32[1179648]{0:T(1024)}), f32[1179648]{0:T(1024)}) %all-reduce.13.cloned.1.call-update) | async-done | bytes 4718608
  (249 shorter events, 72.8 us)
Async XLA Ops:
  7.2 64.4 %all-gather.6.cloned.1.call-start = ((), (), s32[]{:S(2)}) async-start(), calls=%async_computation.1 | async-start | bytes 2433024 | tf_op jit(solution)/shard_map/all_gather | solution.py:121
  8.8 127.6 %all-gather.8.cloned.1.call-start = ((), (), s32[]{:S(2)}) async-start(), calls=%async_computation.2 | async-start | bytes 2228224 | tf_op jit(solution)/shard_map/all_gather | solution.py:124
  10.5 148.9 %all-gather.12.cloned.1.call-start = ((), (), s32[]{:S(2)}) async-start(), calls=%async_computation.5 | async-start | bytes 2162688 | tf_op jit(solution)/shard_map/all_gather | solution.py:140
  77.6 4.2 copy-start.44
  80.2 4.2 copy-start.46
  82.9 3.4 copy-start.50
  87.6 2.3 copy-start.10
  87.6 2.3 copy-start.36
  90.9 42.4 %copy-start.2 = (f32[16,44,512]{2,1,0:T(8,128)}, f32[16,44,512]{2,1,0:T(8,128)S(1)}, u32[]{:S(2)}) copy-start(f32[16,44,512]{2,1,0:T(8,128)S(1)} %get-tuple-element.110) | copy-start | bytes 4325380
  133.4 110.3 %all-gather.10.cloned.1.call-start = ((), (), s32[]{:S(2)}) async-start(), calls=%async_computation.3 | async-start | bytes 10027008 | tf_op jit(solution)/shard_map/all_gather | solution.py:125
  134.6 290.4 %reduce-scatter.4.cloned.1.call-start = ((), (), s32[]{:S(2)}) async-start(), calls=%async_computation.4 | async-start | bytes 4718592 | tf_op jit(solution)/shard_map/reduce_scatter | solution.py:177
  149.0 13.6 %copy-start.66 = (bf16[512,512,1,1]{1,0,2,3:T(8,128)(2,1)}, bf16[512,512,1,1]{1,0,2,3:T(8,128)(2,1)S(1)}, u32[]{:S(2)}) copy-start(bf16[512,512,1,1]{1,0,2,3:T(8,128)(2,1)S(1)} %reshape.400) | copy-start | bytes 1572868
  149.3 12.3 %copy-start.15 = (bf16[512,512,1,1]{1,0,2,3:T(8,128)(2,1)}, bf16[512,512,1,1]{1,0,2,3:T(8,128)(2,1)S(1)}, u32[]{:S(2)}) copy-start(bf16[512,512,1,1]{1,0,2,3:T(8,128)(2,1)S(1)} %reshape.399) | copy-start | bytes 1572868
  282.4 4.2 copy-start.17
  283.9 2.6 copy-start.19
  290.5 2.7 copy-start.21
  290.6 2.7 copy-start.59
  293.6 2.7 copy-start.23
  293.6 2.7 copy-start.58
  296.6 2.7 copy-start.25
  296.6 2.7 copy-start.57
  299.6 2.7 copy-start.27
  299.6 2.7 copy-start.56
  302.7 2.6 copy-start.29
  305.6 2.3 copy-start.6
  305.6 2.4 copy-start.14
  306.9 2.3 copy-start.5
  309.2 9.2 %copy-start.18 = (bf16[512,512,1,1]{1,0,2,3:T(8,128)(2,1)S(1)}, bf16[512,512,1,1]{1,0,2,3:T(8,128)(2,1)}, u32[]{:S(2)}) copy-start(bf16[512,512,1,1]{1,0,2,3:T(8,128)(2,1)} %copy-done.17) | copy-start | bytes 1572868
  322.7 2.7 copy-start.28
  325.4 2.7 copy-start.30
  328.1 2.7 copy-start.32
  330.8 2.7 copy-start.1
  342.2 7.5 copy-start.8
  352.6 267.8 %all-reduce.15.cloned.1.call-start = ((), (), s32[]{:S(2)}) async-start(), calls=%async_computation.7 | async-start | bytes 23068672
  353.0 3.8 copy-start.33
  402.4 369.3 %all-reduce.13.cloned.1.call-start = ((), (), s32[]{:S(2)}) async-start(), calls=%async_computation.6 | async-start | bytes 9437184
  408.0 8.2 %copy-start.4 = (f32[2,16,44,512]{3,2,1,0:T(8,128)S(1)}, f32[2,16,44,512]{3,2,1,0:T(8,128)}, u32[]{:S(2)}) copy-start(f32[2,16,44,512]{3,2,1,0:T(8,128)} %get-tuple-element.95) | copy-start | bytes 8650756
  425.0 46.1 %copy-start.74 = (f32[512]{0:T(512)S(1)}, f32[512]{0:T(512)}, u32[]{:S(2)}) copy-start(f32[512]{0:T(512)} %get-tuple-element.105) | copy-start | bytes 6148
  480.6 139.8 %copy-start.65 = (f32[1,32768]{1,0:T(1,128)S(1)}, f32[1,32768]{1,0:T(1,128)}, u32[]{:S(2)}) copy-start(f32[1,32768]{1,0:T(1,128)} %param.21) | copy-start | bytes 393220
  480.6 139.8 %copy-start.71 = (f32[1,32768]{1,0:T(1,128)S(1)}, f32[1,32768]{1,0:T(1,128)}, u32[]{:S(2)}) copy-start(f32[1,32768]{1,0:T(1,128)} %param.22) | copy-start | bytes 393220
  480.6 139.8 %copy-start.72 = (f32[1,32768]{1,0:T(1,128)S(1)}, f32[1,32768]{1,0:T(1,128)}, u32[]{:S(2)}) copy-start(f32[1,32768]{1,0:T(1,128)} %param.23) | copy-start | bytes 393220
  480.6 142.3 %copy-start.39 = (f32[1,147456]{1,0:T(1,128)S(1)}, f32[1,147456]{1,0:T(1,128)}, u32[]{:S(2)}) copy-start(f32[1,147456]{1,0:T(1,128)} %param.24) | copy-start | bytes 1769476
  480.6 142.3 %copy-start.62 = (f32[1,147456]{1,0:T(1,128)S(1)}, f32[1,147456]{1,0:T(1,128)}, u32[]{:S(2)}) copy-start(f32[1,147456]{1,0:T(1,128)} %param.25) | copy-start | bytes 1769476
  480.6 142.3 %copy-start.63 = (f32[1,147456]{1,0:T(1,128)S(1)}, f32[1,147456]{1,0:T(1,128)}, u32[]{:S(2)}) copy-start(f32[1,147456]{1,0:T(1,128)} %param.26) | copy-start | bytes 1769476
  622.9 6.1 copy-start.53
  636.7 134.9 %copy-start.64 = (f32[36864]{0:T(1024)S(1)}, f32[36864]{0:T(1024)}, u32[]{:S(2)}) copy-start(f32[36864]{0:T(1024)} %param.18) | copy-start | bytes 442372
  636.7 134.9 %copy-start.69 = (f32[36864]{0:T(1024)S(1)}, f32[36864]{0:T(1024)}, u32[]{:S(2)}) copy-start(f32[36864]{0:T(1024)} %param.19) | copy-start | bytes 442372
  636.7 134.9 %copy-start.70 = (f32[36864]{0:T(1024)S(1)}, f32[36864]{0:T(1024)}, u32[]{:S(2)}) copy-start(f32[36864]{0:T(1024)} %param.20) | copy-start | bytes 442372
  (37 other events, 49.6 us)
Sparse Core Ops, SparseCore 0:
  11.5 60.0 all-gather.5
  74.3 40.3 all-gather.7
  133.5 25.9 all-gather.11
  162.2 81.4 all-gather.9
  352.7 41.4 reduce-scatter.3
  402.5 217.8 all-reduce.14
  627.0 144.6 all-reduce.12
where the time goes:
time: 788 us; the launch traced here: 781 us
  waiting for transfers between devices  418 us (53%)
  local copies, waits for them, and re-layouts  127 us (16%)
  matrix products  104 us (13%)
  blocking collectives  80.3 us (10%)
  other arithmetic  33.8 us (4%)
  between operations  16.8 us (2%)
    unnamed x9, waiting for transfers between devices  272 us
    all_gather x1, waiting for transfers between devices, body(): lax.all_gather(head_conv.astype(jnp.bfloat16), 'batch', axis=1, tiled=True)  76 us
    all_gather x1, waiting for transfers between devices, body(): lax.all_gather(trunk_one.astype(jnp.bfloat16), ('batch', 'head'), axis=0,...  59.1 us
    slice x11, local copies, waits for them, and re-layouts, conv_apply(): kernel_low[tap_index]  45.8 us
    psum x1, blocking collectives, body(): lax.psum((local_plain, local_cross), ('batch', 'head'))  41.3 us
    psum x1, blocking collectives, body(): lax.psum((local_sum, local_square), ('batch', 'head'))  39 us
    dot_general x18, matrix products, conv_apply(): jnp.einsum('fhwc,cd->fhwd', window, kernel_low[tap_index], preferred_elem...  37.4 us
    dot_general x18, matrix products, conv_input_grad(): jnp.einsum('fhwd,cd->fhwc', window, kernel_low[tap_index], preferred_elem...  27.3 us
  transfers between devices with their start and end apart: 7, of which 5 were waited for; matrix products, arithmetic and copies ran while one was open for 18% of the time, Pallas kernels for 0%

commit v1 on v0

--- a/solution.py
+++ b/solution.py
@@ -90,6 +90,88 @@
     second_fix = 1.0 - BETA_SECOND**STEP
     update = first_next / first_fix / (jnp.sqrt(second_next / second_fix) + ADAM_EPS)
     return (weight - step_rate * (update + WEIGHT_DECAY * weight), first_next, second_next)
+
+
+def swap_batch(values, bit):
+    return lax.ppermute(values, "batch", [(at, at ^ bit) for at in range(lax.axis_size("batch"))])
+
+
+def swap_head(values):
+    return lax.ppermute(values, "head", [(0, 1), (1, 0)])
+
+
+def pair_up(mine, other, side, axis):
+    first = jnp.where(side == 0, mine, other)
+    second = jnp.where(side == 0, other, mine)
+    return jnp.stack([first, second], axis=axis)
+
+
+def half_of(values, side, axis):
+    return lax.dynamic_index_in_dim(values, side, axis, keepdims=False)
+
+
+def batch_side(bit):
+    return (lax.axis_index("batch") // bit) % 2
+
+
+def far_bits():
+    bits = []
+    bit = lax.axis_size("batch") // 2
+    while bit > 2:
+        bits.append(bit)
+        bit //= 2
+    return bits
+
+
+def sum_batch(values):
+    bit = 1
+    while bit < lax.axis_size("batch"):
+        values = values + swap_batch(values, bit)
+        bit *= 2
+    return values
+
+
+def gather_trunk(rows):
+    count, breadth = rows.shape
+    side_x, side_c, side_h = batch_side(2), batch_side(1), lax.axis_index("head")
+    held = rows[None]
+    for bit in far_bits():
+        other = swap_batch(held, bit)
+        held = pair_up(held, other, batch_side(bit), 1).reshape(-1, count, breadth)
+    half = held.shape[0] // 2
+    one, two = held[:half], held[half:]
+    one_other, two_other = swap_batch(one, 2), swap_head(two)
+    one = pair_up(one, one_other, side_x, 1)
+    two = pair_up(two, two_other, side_h, 1)
+    one_other, two_other = swap_head(one), swap_batch(two, 2)
+    one = pair_up(one, one_other, side_h, 2)
+    two = pair_up(two, two_other, side_x, 1)
+    held = jnp.concatenate([one, two], axis=0)
+    held = pair_up(held, swap_batch(held, 1), side_c, 2)
+    return held.reshape(-1, breadth)
+
+
+def scatter_trunk(values):
+    breadth = values.shape[1]
+    groups = lax.axis_size("batch") // 4
+    side_x, side_c, side_h = batch_side(2), batch_side(1), lax.axis_index("head")
+    held = values.reshape(groups, 2, 2, 2, -1, breadth)
+
+    def give(held, side, axis, swap):
+        sent = half_of(held, 1 - side, axis).astype(jnp.bfloat16)
+        return half_of(held, side, axis) + swap(sent).astype(jnp.float32)
+
+    held = give(held, side_c, 2, lambda v: swap_batch(v, 1))
+    one, two = held[: groups // 2], held[groups // 2 :]
+    one = give(one, side_h, 2, swap_head)
+    two = give(two, side_x, 1, lambda v: swap_batch(v, 2))
+    one = give(one, side_x, 1, lambda v: swap_batch(v, 2))
+    two = give(two, side_h, 1, swap_head)
+    held = jnp.concatenate([one, two], axis=0)
+    for bit in far_bits()[::-1]:
+        held = held.reshape((-1, 2) + held.shape[1:])
+        held = give(held, batch_side(bit), 1, lambda v, bit=bit: swap_batch(v, bit))
+    return held[0]
 
 
 def body(
@@ -111,33 +193,42 @@
 ):
     channels_in = inputs.shape[3]
     channels = norm_params.shape[1]
+    batch = lax.axis_size("batch")
+    side_h = lax.axis_index("head")
     total_count = float(
-        inputs.shape[0]
-        * inputs.shape[1]
-        * inputs.shape[2]
-        * lax.axis_size("batch")
-        * lax.axis_size("head")
-    )
-    one_low = lax.all_gather(trunk_one.astype(jnp.bfloat16), ("batch", "head"), axis=0, tiled=True)
-    kernel_one = one_low.reshape(9, channels_in, channels)
-    attention_low, head_low = (
-        lax.all_gather(attention.astype(jnp.bfloat16), "batch", axis=1, tiled=True),
-        lax.all_gather(head_conv.astype(jnp.bfloat16), "batch", axis=1, tiled=True),
-    )
-    attention_mat = attention_low.reshape(2, channels, channels)
-    head_mat = head_low.reshape(9, channels, channels)
-    field_one = conv_apply(inputs, kernel_one)
-    local_sum = jnp.sum(field_one, axis=(0, 1, 2))
-    local_square = jnp.sum(field_one * field_one, axis=(0, 1, 2))
-    total_sum, total_square = lax.psum((local_sum, local_square), ("batch", "head"))
+        inputs.shape[0] * inputs.shape[1] * inputs.shape[2] * batch * lax.axis_size("head")
+    )
+    att_rows = attention.shape[1] // channels
+    head_rows = head_conv.shape[1] // channels
+    task_low = jnp.concatenate(
+        [
+            attention.reshape(att_rows, channels).astype(jnp.bfloat16),
+            head_conv.reshape(head_rows, channels).astype(jnp.bfloat16),
+        ],
+        axis=0,
+    )
+    task_all = lax.all_gather(task_low, "batch", axis=0, tiled=False)
+    kernel_one = gather_trunk(trunk_one.reshape(-1, channels).astype(jnp.bfloat16)).reshape(
+        9, channels_in, channels
+    )
+    pair_inputs = pair_up(inputs[0], swap_head(inputs[0]), side_h, 0)
+    field_one = conv_apply(pair_inputs, kernel_one)
+    local_sums = jnp.stack(
+        [jnp.sum(field_one, axis=(0, 1, 2)), jnp.sum(field_one * field_one, axis=(0, 1, 2))]
+    )
+    total_sum, total_square = sum_batch(local_sums)
+    attention_mat = task_all[:, :att_rows].reshape(2, channels, channels)
+    head_mat = task_all[:, att_rows:].reshape(9, channels, channels)
     center = total_sum / total_count
     spread = total_square / total_count - center * center
     inverse = lax.rsqrt(spread + EPS_NORM)
     normed = (field_one - center) * inverse
     pre_act = norm_params[0] * normed + norm_params[1]
-    section = jax.nn.gelu(pre_act).astype(jnp.bfloat16)
+    gathered = jax.nn.gelu(pre_act).astype(jnp.bfloat16)
+    section = lax.dynamic_slice_in_dim(gathered, side_h, 1, 0)
+    normed = lax.dynamic_slice_in_dim(normed, side_h, 1, 0)
+    pre_act = lax.dynamic_slice_in_dim(pre_act, side_h, 1, 0)
     shared_out = mean_pool(section.astype(jnp.float32))
-    gathered = lax.all_gather(section, "head", axis=0, tiled=True)
     inner_field = jnp.einsum(
         "fhwc,cd->fhwd", gathered, attention_mat[0], preferred_element_type=jnp.float32
     )
@@ -174,17 +265,27 @@
         )
         + grad_masked * mask_field
     )
-    back_section = lax.psum_scatter(feature_back, "head", scatter_dimension=0, tiled=True)
-    att_grad = jnp.stack([grad_first_att, grad_second_att]).reshape(1, -1)
-    att_share, head_share = (
-        lax.psum_scatter(att_grad, "batch", scatter_dimension=1, tiled=True),
-        lax.psum_scatter(grad_head_kernel.reshape(1, -1), "batch", scatter_dimension=1, tiled=True),
-    )
+    back_other = swap_head(half_of(feature_back, 1 - side_h, 0).astype(jnp.bfloat16))
+    back_section = (half_of(feature_back, side_h, 0) + back_other.astype(jnp.float32))[None]
+    task_grad = jnp.concatenate(
+        [
+            jnp.stack([grad_first_att, grad_second_att]).reshape(batch, att_rows, channels),
+            grad_head_kernel.reshape(batch, head_rows, channels),
+        ],
+        axis=1,
+    ).astype(jnp.bfloat16)
+    task_share = lax.psum_scatter(
+        task_grad.reshape(-1, channels), "batch", scatter_dimension=0, tiled=True
+    ).astype(jnp.float32)
+    att_share = task_share[:att_rows].reshape(1, -1)
+    head_share = task_share[att_rows:].reshape(1, -1)
     grad_section = pool_back(cot_shared.astype(jnp.float32)) + back_section
     grad_pre = gelu_back(pre_act, grad_section)
-    local_plain = jnp.sum(grad_pre, axis=(0, 1, 2))
-    local_cross = jnp.sum(grad_pre * normed, axis=(0, 1, 2))
-    plain_sum, cross_sum = lax.psum((local_plain, local_cross), ("batch", "head"))
+    local_sums = jnp.stack(
+        [jnp.sum(grad_pre, axis=(0, 1, 2)), jnp.sum(grad_pre * normed, axis=(0, 1, 2))]
+    )
+    local_sums = local_sums + swap_head(local_sums)
+    plain_sum, cross_sum = sum_batch(local_sums)
     grad_field = (
         norm_params[0]
         * inverse
@@ -192,9 +293,7 @@
     ).astype(jnp.bfloat16)
     grad_kernel_one = conv_kernel_grad(inputs, grad_field)
     input_grad = conv_input_grad(grad_field, kernel_one)
-    one_share = lax.psum_scatter(
-        grad_kernel_one.reshape(-1), ("batch", "head"), scatter_dimension=0, tiled=True
-    )
+    one_share = scatter_trunk(grad_kernel_one.reshape(-1, channels)).reshape(-1)
     norm_grad = jnp.stack([cross_sum, plain_sum])
     one_new = adamw(trunk_one, trunk_one_first, trunk_one_second, one_share, RATE_MATRIX)
     att_new = adamw(attention, attention_first, attention_second, att_share, RATE_MATRIX)

time: 788 us -> 331 us (0.42)
  waiting for transfers between devices: 418 us -> 101 us
  local copies, waits for them, and re-layouts: 127 us -> 30.4 us
  blocking collectives: 80.3 us -> 0 us
  starting transfers between devices: 1.12 us -> 37.2 us
  other arithmetic: 33.8 us -> 48.4 us
  matrix products: 104 us -> 93.9 us
    unnamed x9 -> x2, waiting for transfers between devices: 272 us -> 0.03 us
    all_gather x4 -> x1, waiting for transfers between devices: 145 us -> 0.01 us  [body(): task_all = lax.all_gather(task_low, 'batch', axis=0, tiled=False)]
    psum x2 -> x0, blocking collectives: 80.3 us -> none  [the longest x1 41.3 us: body(): lax.psum((local_plain, local_cross), ('batch', 'head'))]
    ppermute x0 -> x25, waiting for transfers between devices: none -> 73 us  [the longest x18 45.9 us: swap_batch(): lax.ppermute(values, 'batch', [(at, at ^ bit) for at in range(lax.axis_si...]
    slice x11 -> x3, local copies, waits for them, and re-layouts: 45.8 us -> 5.81 us  [the longest x1 2.81 us: body(): head_mat = task_all[:, att_rows:].reshape(9, channels, channels)]
    ppermute x0 -> x25, starting transfers between devices: none -> 37.1 us  [the longest x18 27 us: swap_batch(): lax.ppermute(values, 'batch', [(at, at ^ bit) for at in range(lax.axis_si...]
    reduce_scatter x1, waiting for transfers between devices: 0.01 us -> 27.9 us  [body(): lax.psum_scatter(task_grad.reshape(-1, channels), 'batch', scatter_dimens...]
    reshape x2 -> x0, local copies, waits for them, and re-layouts: 26 us -> none  [the longest x1 20.6 us: body(): grad_head_kernel.reshape(1, -1)]
  transfers between devices with their start and end apart: 7 -> 27, of which waited for: 5 -> 20; matrix products, arithmetic and copies ran while one was open for 18% -> 23% of each run, Pallas kernels for 0% -> 0%
where the time goes in v1:
time: 331 us; the launch traced here: 326 us
  waiting for transfers between devices  101 us (31%)
  matrix products  93.9 us (28%)
  other arithmetic  48.4 us (15%)
  starting transfers between devices  37.2 us (11%)
  local copies, waits for them, and re-layouts  30.4 us (9%)
  between operations  15.5 us (5%)
    ppermute x18, waiting for transfers between devices, swap_batch(): lax.ppermute(values, 'batch', [(at, at ^ bit) for at in range(lax.axis_si...  45.9 us
    dot_general x18, matrix products, conv_apply(): jnp.einsum('fhwc,cd->fhwd', window, kernel_low[tap_index], preferred_elem...  32.6 us
    dot_general x18, matrix products, conv_input_grad(): jnp.einsum('fhwd,cd->fhwc', window, kernel_low[tap_index], preferred_elem...  32.4 us
    reduce_scatter x1, waiting for transfers between devices, body(): lax.psum_scatter(task_grad.reshape(-1, channels), 'batch', scatter_dimens...  27.9 us
    ppermute x7, waiting for transfers between devices, swap_head(): return lax.ppermute(values, 'head', [(0, 1), (1, 0)])  27.1 us
    ppermute x18, starting transfers between devices, swap_batch(): lax.ppermute(values, 'batch', [(at, at ^ bit) for at in range(lax.axis_si...  27 us
    dot_general x18, matrix products, conv_kernel_grad(): jnp.einsum('fhwc,fhwd->cd', window, grad_low, preferred_element_type=jnp....  16 us
    ppermute x7, starting transfers between devices, swap_head(): return lax.ppermute(values, 'head', [(0, 1), (1, 0)])  10.1 us
  transfers between devices with their start and end apart: 27, of which 20 were waited for; matrix products, arithmetic and copies ran while one was open for 23% of the time, Pallas kernels for 0%

profile of v1, /device:TPU:0, one launch (start us, length us, event | category | flops | bytes accessed | tf_op | source)
XLA Modules:
  0.0 326.3 jit_solution(10344189265194205730)
XLA Ops:
  7.2 7.1 %convert_reduce_fusion = bf16[147456]{0:T(1024)(128)(2,1)S(1)} fusion(f32[1,147456]{1,0:T(1,128)} %param.24), kind=kLoop, calls=%fused_computation.228 | loop fusion | flops 147456 | bytes 884736 | tf_op jit(solution)/shard_map/convert_element_type | solution.py:206
  16.7 4.1 %collective-permute-start.1 = (bf16[1,72,512]{2,1,0:T(8,128)(2,1)S(1)}, bf16[1,72,512]{2,1,0:T(8,128)(2,1)S(1)}, u32[]{:S(2)}, u32[]{:S(2)}) collective-permute-start(bf16[1,72,512]{2,1,0:T(8,128)(2,1)S(1)} %convert_element_type.151), channel_id=1, source_target_pairs={{0,16},{2,18},{4,20},{6,22},{8,24},{10,26},{12,28},{14,30},{16,0},... | collective-permute-start | bytes 221192 | tf_op jit(solution)/shard_map/ppermute | solution.py:96
  20.8 3.9 %collective-permute-done.1 = bf16[1,72,512]{2,1,0:T(8,128)(2,1)S(1)} collective-permute-done((bf16[1,72,512]{2,1,0:T(8,128)(2,1)S(1)}, bf16[1,72,512]{2,1,0:T(8,128)(2,1)S(1)}, u32[]{:S(2)}, u32[]{:S(2)}) %collective-permute-start.1) | collective-permute-done | bytes 73760 | tf_op jit(solution)/shard_map/ppermute | solution.py:96
  25.5 4.5 %collective-permute-done.2 = bf16[2,72,512]{2,1,0:T(8,128)(2,1)S(1)} collective-permute-done((bf16[2,72,512]{2,1,0:T(8,128)(2,1)S(1)}, bf16[2,72,512]{2,1,0:T(8,128)(2,1)S(1)}, u32[]{:S(2)}, u32[]{:S(2)}) %collective-permute-start.2) | collective-permute-done | bytes 147488 | tf_op jit(solution)/shard_map/ppermute | solution.py:96
  33.4 1.9 collective-permute-done.5
  40.1 3.4 %collective-permute-done.6 = bf16[2,2,72,512]{3,2,1,0:T(8,128)(2,1)S(1)} collective-permute-done((bf16[2,2,72,512]{3,2,1,0:T(8,128)(2,1)S(1)}, bf16[2,2,72,512]{3,2,1,0:T(8,128)(2,1)S(1)}, u32[]{:S(2)}, u32[]{:S(2)}) %collective-permute-start.6) | collective-permute-done | bytes 294944 | tf_op jit(solution)/shard_map/ppermute | solution.py:96
  43.5 1.9 collective-permute-done.4
  48.2 10.3 %collective-permute-done = bf16[16,44,256]{2,1,0:T(8,128)(2,1)} collective-permute-done((bf16[16,44,256]{2,1,0:T(8,128)(2,1)S(1)}, bf16[16,44,256]{2,1,0:T(8,128)(2,1)}, u32[]{:S(2)}, u32[]{:S(2)}) %collective-permute-start) | collective-permute-done | bytes 360480 | tf_op jit(solution)/shard_map/ppermute | solution.py:100
  59.7 2.7 pad_slice_fusion.48
  67.8 3.1 fusion.247
  73.8 2.1 collective-permute-done.9
  77.4 2.1 collective-permute-done.10
  79.5 7.6 %collective-permute-start.11 = (f32[2,512]{1,0:T(2,128)S(1)}, f32[2,512]{1,0:T(2,128)S(1)}, u32[]{:S(2)}, u32[]{:S(2)}) collective-permute-start(f32[2,512]{1,0:T(2,128)S(1)} %add.380), channel_id=1, source_target_pairs={{0,16},{2,18},{4,20},{6,22},{8,24},{10,26},{12,28},{14,30},{16,0},... | collective-permute-start | bytes 12296 | tf_op jit(solution)/shard_map/ppermute | solution.py:96
  89.2 2.1 broadcast_in_dim.7
  91.9 5.7 %fusion.25 = (bf16[2,16,44,512]{3,1,2,0:T(8,128)(2,1)S(1)}, f32[2,16,44,512]{3,1,2,0:T(8,128)}, f32[2,16,44,512]{3,1,2,0:T(8,128)}) fusion(f32[512]{0:T(512)S(1)} %bitcast.675, f32[512]{0:T(512)S(1)} %bitcast.670, f32[512]{0:T(512)S(1)} %get-tuple-element.92, f32[2,16,44,512]{3,1,2,0:T(8,128)} %get-tuple-element.146, f32[512]{0:T(512)S(1)} %bitcast.672), kind=kLoop, calls=%fused_computation.49 | loop fusion | flops 9371648 | bytes 10100736 | tf_op jit(solution)/shard_map/convert_element_type | solution.py:227
  98.9 2.3 reshape.378
  103.1 2.8 slice.337
  108.2 3.2 fusion
  114.1 2.6 fusion.130
  116.7 2.5 fusion.88
  119.2 2.6 fusion.87
  121.7 2.6 fusion.85
  124.3 2.4 fusion.86
  126.8 2.5 broadcast_in_dim.8
  129.3 9.6 %fusion.17 = (bf16[2,16,44,512]{3,1,2,0:T(8,128)(2,1)S(1)}, f32[2,16,44,512]{3,1,2,0:T(8,128)}) fusion(f32[2,16,44,512]{3,0,2,1:T(2,128)} %bitcast.637, bf16[9,512,512]{2,1,0:T(8,128)(2,1)S(1)} %bitcast.598, bf16[2,16,44,512]{3,1,2,0:T(8,128)(2,1)S(1)} %get-tuple-element.147, f32[2,16,44,512]{3,1,2,0:T(8,128)S(1)} %fusion.91, ...), kind=kOutput, calls=%fused_computation.41 | convolution fusion | flops 759103488 | bytes 32243712 | tf_op jit(solution)/shard_map/fhwc,cd->fhwd/dot_general | solution.py:31
  140.8 2.5 fusion.36
  143.4 2.5 fusion.129
  145.9 2.5 fusion.35
  148.4 2.5 fusion.34
  150.9 2.6 fusion.32
  153.5 2.5 fusion.33
  157.8 9.6 %fusion.3 = (bf16[2,16,44,512]{3,1,2,0:T(8,128)(2,1)S(1)}, f32[2,16,44,512]{3,1,2,0:T(8,128)}) fusion(f32[2,16,44,512]{3,1,2,0:T(8,128)} %get-tuple-element.148, bf16[2,16,44,512]{3,1,2,0:T(8,128)(2,1)S(1)} %get-tuple-element.94, bf16[9,512,512]{2,1,0:T(8,128)(2,1)S(1)} %bitcast.607, bf16[2,16,44,512]{3,1,2,0:T(8,128)(2,1)S(1)} %get-tuple-element.99, ...), kind=kOutput, calls=%fused_computation.27 | convolution fusion | flops 748290048 | bytes 33685504 | tf_op jit(solution)/shard_map/fhwd,cd->fhwc/dot_general | solution.py:48
  167.5 4.1 %fusion.10 = bf16[2,16,44,512]{3,1,2,0:T(8,128)(2,1)S(1)} fusion(f32[2,16,44,512]{3,1,2,0:T(8,128)} %copy-done.12, bf16[2,16,44,512]{3,1,2,0:T(8,128)(2,1)S(1)} %get-tuple-element.149, bf16[512,512,1,1]{1,0,3,2:T(8,128)(2,1)S(1)} %bitcast.654), kind=kOutput, calls=%fused_computation.34 | convolution fusion | flops 752615424 | bytes 6291456 | tf_op jit(solution)/shard_map/fhwd,cd->fhwc/dot_general | solution.py:255
  171.6 2.1 fusion.82
  184.9 8.6 %collective-permute-done.12 = bf16[16,44,512]{2,0,1:T(8,128)(2,1)S(1)} collective-permute-done((bf16[16,44,512]{2,0,1:T(8,128)(2,1)S(1)}, bf16[16,44,512]{2,0,1:T(8,128)(2,1)S(1)}, u32[]{:S(2)}, u32[]{:S(2)}) %collective-permute-start.12) | collective-permute-done | bytes 720928 | tf_op jit(solution)/shard_map/ppermute | solution.py:100
  193.6 2.3 fusion.248
  200.7 2.1 copy-done.8
  202.8 4.0 %copy.115 = f32[2,16,44,512]{3,0,2,1:T(2,128)} copy(f32[2,16,44,512]{3,1,2,0:T(8,128)S(1)} %copy-done.5) | data formatting | bytes 5767168 | tf_op jit(solution)/shard_map/mul | solution.py:243
  206.8 4.3 %reduce_sum.57 = f32[2,8,22,512]{3,0,2,1:T(2,128)} reduce(f32[2,8,2,22,2,512]{5,0,4,3,2,1:T(2,128)} %bitcast.636, f32[]{:T(128)} %constant.212.clone.1), dimensions={2,4}, to_apply=%region_3.4 | reduce | flops 540672 | bytes 3604484 | tf_op jit(solution)/shard_map/reduce_sum | solution.py:71
  218.8 5.3 %pad_maximum_fusion = bf16[16,352,512]{2,1,0:T(8,128)(2,1)} fusion(bf16[16,288,512]{2,1,0:T(8,128)(2,1)} %bitcast.642, bf16[16,64,512]{2,1,0:T(8,128)(2,1)S(1)} %bitcast.645), kind=kLoop, calls=%fused_computation | loop fusion | flops 11534336 | bytes 11534336 | tf_op jit(solution)/shard_map/concatenate | solution.py:270
  234.1 2.1 fusion.109
  244.4 6.4 %collective-permute-done.21 = bf16[2,2,72,512]{3,2,1,0:T(8,128)(2,1)S(1)} collective-permute-done((bf16[2,2,72,512]{3,2,1,0:T(8,128)(2,1)S(1)}, bf16[2,2,72,512]{3,2,1,0:T(8,128)(2,1)S(1)}, u32[]{:S(2)}, u32[]{:S(2)}) %collective-permute-start.21) | collective-permute-done | bytes 294944 | tf_op jit(solution)/shard_map/ppermute | solution.py:96
  253.6 2.9 collective-permute-done.22
  260.2 10.6 %collective-permute-done.23 = bf16[2,72,512]{2,1,0:T(8,128)(2,1)S(1)} collective-permute-done((bf16[2,72,512]{2,1,0:T(8,128)(2,1)S(1)}, bf16[2,72,512]{2,1,0:T(8,128)(2,1)S(1)}, u32[]{:S(2)}, u32[]{:S(2)}) %collective-permute-start.23) | collective-permute-done | bytes 147488 | tf_op jit(solution)/shard_map/ppermute | solution.py:96
  270.9 2.0 collective-permute-start.24
  274.7 6.7 %collective-permute-done.24 = bf16[1,72,512]{2,1,0:T(8,128)(2,1)S(1)} collective-permute-done((bf16[1,72,512]{2,1,0:T(8,128)(2,1)S(1)}, bf16[1,72,512]{2,1,0:T(8,128)(2,1)S(1)}, u32[]{:S(2)}, u32[]{:S(2)}) %collective-permute-start.24) | collective-permute-done | bytes 73760 | tf_op jit(solution)/shard_map/ppermute | solution.py:96
  282.4 27.9 %reduce-scatter.2.cloned.1.call-done = bf16[352,512]{1,0:T(8,128)(2,1)} async-done(((bf16[5632,512]{1,0:T(8,128)(2,1)}), bf16[352,512]{1,0:T(8,128)(2,1)}) %reduce-scatter.2.cloned.1.call-update) | async-done | bytes 360464 | tf_op jit(solution)/shard_map/reduce_scatter | solution.py:277
  313.9 5.1 %multiply_subtract_fusion = (f32[1,147456]{1,0:T(1,128)}, f32[1,147456]{1,0:T(1,128)}, f32[1,147456]{1,0:T(1,128)}) fusion(f32[1,147456]{1,0:T(1,128)S(1)} %copy-done.14, f32[1,147456]{1,0:T(1,128)S(1)} %bitcast.648, f32[1,147456]{1,0:T(1,128)S(1)} %copy-done.17, f32[1,147456]{1,0:T(1,128)S(1)} %copy-done.18), kind=kLoop, calls=%fused_computation.225 | loop fusion | flops 2211840 | bytes 4128768 | tf_op jit(solution)/shard_map/sub | solution.py:92
  (230 shorter events, 93.8 us)
Async XLA Ops:
  7.2 9.5 %copy-start.15 = (f32[36864]{0:T(1024)S(1)}, f32[36864]{0:T(1024)}, u32[]{:S(2)}) copy-start(f32[36864]{0:T(1024)} %param.18) | copy-start | bytes 442372
  7.2 95.9 %all-gather.3.cloned.1.call-start = ((), (), s32[]{:S(2)}) async-start(), calls=%async_computation.2 | async-start | bytes 6127616 | tf_op jit(solution)/shard_map/all_gather | solution.py:210
  16.6 293.8 %reduce-scatter.2.cloned.1.call-start = ((), (), s32[]{:S(2)}) async-start(), calls=%async_computation.1 | async-start | bytes 6127616 | tf_op jit(solution)/shard_map/reduce_scatter | solution.py:277
  16.7 8.0 %collective-permute-start.1 = (bf16[1,72,512]{2,1,0:T(8,128)(2,1)S(1)}, bf16[1,72,512]{2,1,0:T(8,128)(2,1)S(1)}, u32[]{:S(2)}, u32[]{:S(2)}) collective-permute-start(bf16[1,72,512]{2,1,0:T(8,128)(2,1)S(1)} %convert_element_type.151), channel_id=1, source_target_pairs={{0,16},{2,18},{4,20},{6,22},{8,24},{10,26},{12,28},{14,30},{16,0},... | collective-permute-start | bytes 221192 | tf_op jit(solution)/shard_map/ppermute | solution.py:96
  24.8 5.2 %collective-permute-start.2 = (bf16[2,72,512]{2,1,0:T(8,128)(2,1)S(1)}, bf16[2,72,512]{2,1,0:T(8,128)(2,1)S(1)}, u32[]{:S(2)}, u32[]{:S(2)}) collective-permute-start(bf16[2,72,512]{2,1,0:T(8,128)(2,1)S(1)} %maximum_bitcast_fusion), channel_id=1, source_target_pairs={{0,8},{2,10},{4,12},{6,14},{8,0},{10,2},{12,4},{14,6},{16,24},{18,... | collective-permute-start | bytes 442376 | tf_op jit(solution)/shard_map/ppermute | solution.py:96
  30.1 5.2 %collective-permute-start.5 = (bf16[2,72,512]{2,1,0:T(8,128)(2,1)S(1)}, bf16[2,72,512]{2,1,0:T(8,128)(2,1)S(1)}, u32[]{:S(2)}, u32[]{:S(2)}) collective-permute-start(bf16[2,72,512]{2,1,0:T(8,128)(2,1)S(1)} %get-tuple-element.132), channel_id=1, source_target_pairs={{0,1},{1,0},{2,3},{3,2},{4,5},{5,4},{6,7},{7,6},{8,9},{9,8},{10,11... | collective-permute-start | bytes 442376 | tf_op jit(solution)/shard_map/ppermute | solution.py:100
  31.9 6.7 %collective-permute-start.3 = (bf16[2,72,512]{2,1,0:T(8,128)(2,1)S(1)}, bf16[2,72,512]{2,1,0:T(8,128)(2,1)S(1)}, u32[]{:S(2)}, u32[]{:S(2)}) collective-permute-start(bf16[2,72,512]{2,1,0:T(8,128)(2,1)S(1)} %get-tuple-element.131), channel_id=1, source_target_pairs={{0,4},{2,6},{4,0},{6,2},{8,12},{10,14},{12,8},{14,10},{16,20},{18,... | collective-permute-start | bytes 442376 | tf_op jit(solution)/shard_map/ppermute | solution.py:96
  35.3 11.3 %copy-start.9 = (bf16[1,16,44,256]{3,1,2,0:T(8,128)(2,1)S(1)}, bf16[1,16,44,256]{3,1,2,0:T(8,128)(2,1)}, u32[]{:S(2)}) copy-start(bf16[1,16,44,256]{3,1,2,0:T(8,128)(2,1)} %param.15) | copy-start | bytes 1081348
  35.4 8.1 %collective-permute-start.6 = (bf16[2,2,72,512]{3,2,1,0:T(8,128)(2,1)S(1)}, bf16[2,2,72,512]{3,2,1,0:T(8,128)(2,1)S(1)}, u32[]{:S(2)}, u32[]{:S(2)}) collective-permute-start(bf16[2,2,72,512]{3,2,1,0:T(8,128)(2,1)S(1)} %pad_maximum_fusion.8), channel_id=1, source_target_pairs={{0,4},{2,6},{4,0},{6,2},{8,12},{10,14},{12,8},{14,10},{16,20},{18,... | collective-permute-start | bytes 884744 | tf_op jit(solution)/shard_map/ppermute | solution.py:96
  38.7 6.8 %collective-permute-start.4 = (bf16[2,2,72,512]{3,2,0,1:T(8,128)(2,1)S(1)}, bf16[2,2,72,512]{3,2,0,1:T(8,128)(2,1)S(1)}, u32[]{:S(2)}, u32[]{:S(2)}) collective-permute-start(bf16[2,2,72,512]{3,2,0,1:T(8,128)(2,1)S(1)} %pad_maximum_fusion.7), channel_id=1, source_target_pairs={{0,1},{1,0},{2,3},{3,2},{4,5},{5,4},{6,7},{7,6},{8,9},{9,8},{10,11... | collective-permute-start | bytes 884744 | tf_op jit(solution)/shard_map/ppermute | solution.py:100
  46.7 15.8 %collective-permute-start.7 = (bf16[4,2,2,72,512]{4,3,2,1,0:T(8,128)(2,1)}, bf16[4,2,2,72,512]{4,3,2,1,0:T(8,128)(2,1)S(1)}, u32[]{:S(2)}, u32[]{:S(2)}) collective-permute-start(bf16[4,2,2,72,512]{4,3,2,1,0:T(8,128)(2,1)} %maximum_maximum_fusion), channel_id=1, source_target_pairs={{0,2},{2,0},{4,6},{6,4},{8,10},{10,8},{12,14},{14,12},{16,18},{18,... | collective-permute-start | bytes 3538952 | tf_op jit(solution)/shard_map/ppermute | solution.py:96
  46.8 11.7 %collective-permute-start = (bf16[16,44,256]{2,1,0:T(8,128)(2,1)S(1)}, bf16[16,44,256]{2,1,0:T(8,128)(2,1)}, u32[]{:S(2)}, u32[]{:S(2)}) collective-permute-start(bf16[16,44,256]{2,1,0:T(8,128)(2,1)S(1)} %bitcast.655), channel_id=1, source_target_pairs={{0,1},{1,0},{2,3},{3,2},{4,5},{5,4},{6,7},{7,6},{8,9},{9,8},{10,11... | collective-permute-start | bytes 1081352 | tf_op jit(solution)/shard_map/ppermute | solution.py:100
  67.7 9.7 %copy-start.24 = (bf16[1,8,22,512]{3,1,2,0:T(8,128)(2,1)S(1)}, bf16[1,8,22,512]{3,1,2,0:T(8,128)(2,1)}, u32[]{:S(2)}) copy-start(bf16[1,8,22,512]{3,1,2,0:T(8,128)(2,1)} %param.16) | copy-start | bytes 540676
  67.8 19.3 %copy-start.29 = (f32[2,512]{1,0:T(2,128)S(1)}, f32[2,512]{1,0:T(2,128)}, u32[]{:S(2)}) copy-start(f32[2,512]{1,0:T(2,128)} %param.27) | copy-start | bytes 12292
  70.9 1.2 collective-permute-start.8
  72.2 3.7 %collective-permute-start.9 = (f32[2,512]{1,0:T(2,128)S(1)}, f32[2,512]{1,0:T(2,128)S(1)}, u32[]{:S(2)}, u32[]{:S(2)}) collective-permute-start(f32[2,512]{1,0:T(2,128)S(1)} %fusion.246), channel_id=1, source_target_pairs={{0,4},{2,6},{4,0},{6,2},{8,12},{10,14},{12,8},{14,10},{16,20},{18,... | collective-permute-start | bytes 12296 | tf_op jit(solution)/shard_map/ppermute | solution.py:96
  75.9 3.7 %collective-permute-start.10 = (f32[2,512]{1,0:T(2,128)S(1)}, f32[2,512]{1,0:T(2,128)S(1)}, u32[]{:S(2)}, u32[]{:S(2)}) collective-permute-start(f32[2,512]{1,0:T(2,128)S(1)} %fusion.284), channel_id=1, source_target_pairs={{0,8},{2,10},{4,12},{6,14},{8,0},{10,2},{12,4},{14,6},{16,24},{18,... | collective-permute-start | bytes 12296 | tf_op jit(solution)/shard_map/ppermute | solution.py:96
  79.5 11.8 %collective-permute-start.11 = (f32[2,512]{1,0:T(2,128)S(1)}, f32[2,512]{1,0:T(2,128)S(1)}, u32[]{:S(2)}, u32[]{:S(2)}) collective-permute-start(f32[2,512]{1,0:T(2,128)S(1)} %add.380), channel_id=1, source_target_pairs={{0,16},{2,18},{4,20},{6,22},{8,24},{10,26},{12,28},{14,30},{16,0},... | collective-permute-start | bytes 12296 | tf_op jit(solution)/shard_map/ppermute | solution.py:96
  171.6 7.3 %slice-start = ((s8[4718592]{0:T(1024)(128)(4,1)}), s8[4194304]{0:T(1024)(128)(4,1)S(1)}, s32[]{:S(2)}) async-start(s8[4718592]{0:T(1024)(128)(4,1)} %bitcast.640), calls=%async_computation.3 | async-start | bytes 8388608
  177.6 15.9 %collective-permute-start.12 = (bf16[16,44,512]{2,0,1:T(8,128)(2,1)S(1)}, bf16[16,44,512]{2,0,1:T(8,128)(2,1)S(1)}, u32[]{:S(2)}, u32[]{:S(2)}) collective-permute-start(bf16[16,44,512]{2,0,1:T(8,128)(2,1)S(1)} %fusion.101), channel_id=1, source_target_pairs={{0,1},{1,0},{2,3},{3,2},{4,5},{5,4},{6,7},{7,6},{8,9},{9,8},{10,11... | collective-permute-start | bytes 2162696 | tf_op jit(solution)/shard_map/ppermute | solution.py:100
  183.9 9.7 %copy-start.2 = (f32[2,16,44,512]{3,1,2,0:T(8,128)S(1)}, f32[2,16,44,512]{3,1,2,0:T(8,128)}, u32[]{:S(2)}) copy-start(f32[2,16,44,512]{3,1,2,0:T(8,128)} %get-tuple-element.96) | copy-start | bytes 8650756
  183.9 9.6 %copy-start.6 = (f32[2,16,44,512]{3,1,2,0:T(8,128)S(1)}, f32[2,16,44,512]{3,1,2,0:T(8,128)}, u32[]{:S(2)}) copy-start(f32[2,16,44,512]{3,1,2,0:T(8,128)} %get-tuple-element.95) | copy-start | bytes 8650756
  183.9 9.6 %copy-start.7 = (f32[16,44,512]{2,0,1:T(8,128)S(1)}, f32[16,44,512]{2,0,1:T(8,128)}, u32[]{:S(2)}) copy-start(f32[16,44,512]{2,0,1:T(8,128)} %broadcast_in_dim.7) | copy-start | bytes 4325380
  195.9 3.7 %collective-permute-start.13 = (f32[2,512]{1,0:T(2,128)S(1)}, f32[2,512]{1,0:T(2,128)S(1)}, u32[]{:S(2)}, u32[]{:S(2)}) collective-permute-start(f32[2,512]{1,0:T(2,128)S(1)} %pad_maximum_fusion.11), channel_id=1, source_target_pairs={{0,1},{1,0},{2,3},{3,2},{4,5},{5,4},{6,7},{7,6},{8,9},{9,8},{10,11... | collective-permute-start | bytes 12296 | tf_op jit(solution)/shard_map/ppermute | solution.py:100
  199.6 11.5 %collective-permute-start.14 = (f32[2,512]{1,0:T(2,128)S(1)}, f32[2,512]{1,0:T(2,128)S(1)}, u32[]{:S(2)}, u32[]{:S(2)}) collective-permute-start(f32[2,512]{1,0:T(2,128)S(1)} %fusion.245), channel_id=1, source_target_pairs={{0,2},{2,0},{4,6},{6,4},{8,10},{10,8},{12,14},{14,12},{16,18},{18,... | collective-permute-start | bytes 12296 | tf_op jit(solution)/shard_map/ppermute | solution.py:96
  206.8 9.7 %copy-start.20 = (bf16[1,512,512]{2,1,0:T(8,128)(2,1)S(1)}, bf16[1,512,512]{2,1,0:T(8,128)(2,1)}, u32[]{:S(2)}) copy-start(bf16[1,512,512]{2,1,0:T(8,128)(2,1)} %fusion.82) | copy-start | bytes 1572868
  211.1 3.7 %collective-permute-start.15 = (f32[2,512]{1,0:T(2,128)S(1)}, f32[2,512]{1,0:T(2,128)S(1)}, u32[]{:S(2)}, u32[]{:S(2)}) collective-permute-start(f32[2,512]{1,0:T(2,128)S(1)} %fusion.283), channel_id=1, source_target_pairs={{0,4},{2,6},{4,0},{6,2},{8,12},{10,14},{12,8},{14,10},{16,20},{18,... | collective-permute-start | bytes 12296 | tf_op jit(solution)/shard_map/ppermute | solution.py:96
  214.8 3.6 %collective-permute-start.16 = (f32[2,512]{1,0:T(2,128)S(1)}, f32[2,512]{1,0:T(2,128)S(1)}, u32[]{:S(2)}, u32[]{:S(2)}) collective-permute-start(f32[2,512]{1,0:T(2,128)S(1)} %add.420), channel_id=1, source_target_pairs={{0,8},{2,10},{4,12},{6,14},{8,0},{10,2},{12,4},{14,6},{16,24},{18,... | collective-permute-start | bytes 12296 | tf_op jit(solution)/shard_map/ppermute | solution.py:96
  218.4 6.8 %collective-permute-start.17 = (f32[2,512]{1,0:T(2,128)S(1)}, f32[2,512]{1,0:T(2,128)S(1)}, u32[]{:S(2)}, u32[]{:S(2)}) collective-permute-start(f32[2,512]{1,0:T(2,128)S(1)} %add.421), channel_id=1, source_target_pairs={{0,16},{2,18},{4,20},{6,22},{8,24},{10,26},{12,28},{14,30},{16,0},... | collective-permute-start | bytes 12296 | tf_op jit(solution)/shard_map/ppermute | solution.py:96
  234.0 6.7 %collective-permute-start.18 = (bf16[4,2,2,72,512]{4,3,2,1,0:T(8,128)(2,1)S(1)}, bf16[4,2,2,72,512]{4,3,2,1,0:T(8,128)(2,1)S(1)}, u32[]{:S(2)}, u32[]{:S(2)}) collective-permute-start(bf16[4,2,2,72,512]{4,3,2,1,0:T(8,128)(2,1)S(1)} %fusion.84), channel_id=1, source_target_pairs={{0,2},{2,0},{4,6},{6,4},{8,10},{10,8},{12,14},{14,12},{16,18},{18,... | collective-permute-start | bytes 3538952 | tf_op jit(solution)/shard_map/ppermute | solution.py:96
  241.4 9.5 %collective-permute-start.21 = (bf16[2,2,72,512]{3,2,1,0:T(8,128)(2,1)S(1)}, bf16[2,2,72,512]{3,2,1,0:T(8,128)(2,1)S(1)}, u32[]{:S(2)}, u32[]{:S(2)}) collective-permute-start(bf16[2,2,72,512]{3,2,1,0:T(8,128)(2,1)S(1)} %fusion.157), channel_id=1, source_target_pairs={{0,4},{2,6},{4,0},{6,2},{8,12},{10,14},{12,8},{14,10},{16,20},{18,... | collective-permute-start | bytes 884744 | tf_op jit(solution)/shard_map/ppermute | solution.py:96
  242.6 16.9 %copy-start.30 = (f32[2,512]{1,0:T(2,128)S(1)}, f32[2,512]{1,0:T(2,128)}, u32[]{:S(2)}) copy-start(f32[2,512]{1,0:T(2,128)} %param.27) | copy-start | bytes 12292
  242.6 16.9 %copy-start.32 = (f32[2,512]{1,0:T(2,128)S(1)}, f32[2,512]{1,0:T(2,128)}, u32[]{:S(2)}) copy-start(f32[2,512]{1,0:T(2,128)} %param.28) | copy-start | bytes 12292
  242.6 16.9 %copy-start.33 = (f32[2,512]{1,0:T(2,128)S(1)}, f32[2,512]{1,0:T(2,128)}, u32[]{:S(2)}) copy-start(f32[2,512]{1,0:T(2,128)} %param.29) | copy-start | bytes 12292
  242.6 9.6 %collective-permute-start.19 = (bf16[2,2,72,512]{3,2,0,1:T(8,128)(2,1)S(1)}, bf16[2,2,72,512]{3,2,0,1:T(8,128)(2,1)S(1)}, u32[]{:S(2)}, u32[]{:S(2)}) collective-permute-start(bf16[2,2,72,512]{3,2,0,1:T(8,128)(2,1)S(1)} %fusion.158), channel_id=1, source_target_pairs={{0,1},{1,0},{2,3},{3,2},{4,5},{5,4},{6,7},{7,6},{8,9},{9,8},{10,11... | collective-permute-start | bytes 884744 | tf_op jit(solution)/shard_map/ppermute | solution.py:100
  251.0 5.5 %collective-permute-start.22 = (bf16[2,72,512]{2,1,0:T(8,128)(2,1)S(1)}, bf16[2,72,512]{2,1,0:T(8,128)(2,1)S(1)}, u32[]{:S(2)}, u32[]{:S(2)}) collective-permute-start(bf16[2,72,512]{2,1,0:T(8,128)(2,1)S(1)} %fusion.205), channel_id=1, source_target_pairs={{0,1},{1,0},{2,3},{3,2},{4,5},{5,4},{6,7},{7,6},{8,9},{9,8},{10,11... | collective-permute-start | bytes 442376 | tf_op jit(solution)/shard_map/ppermute | solution.py:100
  252.4 5.2 %collective-permute-start.20 = (bf16[2,72,512]{2,1,0:T(8,128)(2,1)S(1)}, bf16[2,72,512]{2,1,0:T(8,128)(2,1)S(1)}, u32[]{:S(2)}, u32[]{:S(2)}) collective-permute-start(bf16[2,72,512]{2,1,0:T(8,128)(2,1)S(1)} %fusion.204), channel_id=1, source_target_pairs={{0,4},{2,6},{4,0},{6,2},{8,12},{10,14},{12,8},{14,10},{16,20},{18,... | collective-permute-start | bytes 442376 | tf_op jit(solution)/shard_map/ppermute | solution.py:96
  257.7 23.8 %copy-start.16 = (f32[36864]{0:T(1024)S(1)}, f32[36864]{0:T(1024)}, u32[]{:S(2)}) copy-start(f32[36864]{0:T(1024)} %param.18) | copy-start | bytes 442372
  257.7 23.8 %copy-start.25 = (f32[36864]{0:T(1024)S(1)}, f32[36864]{0:T(1024)}, u32[]{:S(2)}) copy-start(f32[36864]{0:T(1024)} %param.19) | copy-start | bytes 442372
  257.7 23.8 %copy-start.26 = (f32[36864]{0:T(1024)S(1)}, f32[36864]{0:T(1024)}, u32[]{:S(2)}) copy-start(f32[36864]{0:T(1024)} %param.20) | copy-start | bytes 442372
  257.7 13.1 %collective-permute-start.23 = (bf16[2,72,512]{2,1,0:T(8,128)(2,1)S(1)}, bf16[2,72,512]{2,1,0:T(8,128)(2,1)S(1)}, u32[]{:S(2)}, u32[]{:S(2)}) collective-permute-start(bf16[2,72,512]{2,1,0:T(8,128)(2,1)S(1)} %fusion.206), channel_id=1, source_target_pairs={{0,8},{2,10},{4,12},{6,14},{8,0},{10,2},{12,4},{14,6},{16,24},{18,... | collective-permute-start | bytes 442376 | tf_op jit(solution)/shard_map/ppermute | solution.py:96
  270.9 10.6 %collective-permute-start.24 = (bf16[1,72,512]{2,1,0:T(8,128)(2,1)S(1)}, bf16[1,72,512]{2,1,0:T(8,128)(2,1)S(1)}, u32[]{:S(2)}, u32[]{:S(2)}) collective-permute-start(bf16[1,72,512]{2,1,0:T(8,128)(2,1)S(1)} %dynamic-slice_convert_fusion.7), channel_id=1, source_target_pairs={{0,16},{2,18},{4,20},{6,22},{8,24},{10,26},{12,28},{14,30},{16,0},... | collective-permute-start | bytes 221192 | tf_op jit(solution)/shard_map/ppermute | solution.py:96
  274.7 37.5 %copy-start.19 = (f32[1,32768]{1,0:T(1,128)S(1)}, f32[1,32768]{1,0:T(1,128)}, u32[]{:S(2)}) copy-start(f32[1,32768]{1,0:T(1,128)} %param.21) | copy-start | bytes 393220
  274.7 37.5 %copy-start.27 = (f32[1,32768]{1,0:T(1,128)S(1)}, f32[1,32768]{1,0:T(1,128)}, u32[]{:S(2)}) copy-start(f32[1,32768]{1,0:T(1,128)} %param.22) | copy-start | bytes 393220
  274.7 37.5 %copy-start.28 = (f32[1,32768]{1,0:T(1,128)S(1)}, f32[1,32768]{1,0:T(1,128)}, u32[]{:S(2)}) copy-start(f32[1,32768]{1,0:T(1,128)} %param.23) | copy-start | bytes 393220
  281.6 32.4 %copy-start.14 = (f32[1,147456]{1,0:T(1,128)S(1)}, f32[1,147456]{1,0:T(1,128)}, u32[]{:S(2)}) copy-start(f32[1,147456]{1,0:T(1,128)} %param.24) | copy-start | bytes 1769476
  281.6 32.3 %copy-start.17 = (f32[1,147456]{1,0:T(1,128)S(1)}, f32[1,147456]{1,0:T(1,128)}, u32[]{:S(2)}) copy-start(f32[1,147456]{1,0:T(1,128)} %param.25) | copy-start | bytes 1769476
  281.6 32.3 %copy-start.18 = (f32[1,147456]{1,0:T(1,128)S(1)}, f32[1,147456]{1,0:T(1,128)}, u32[]{:S(2)}) copy-start(f32[1,147456]{1,0:T(1,128)} %param.26) | copy-start | bytes 1769476
  (15 other events, 43.5 us)
Sparse Core Ops, SparseCore 0:
  16.7 62.2 all-gather.2
  225.4 84.9 reduce-scatter.1
